TPU v7x, 32 devices: a whole 2x2x4 slice. The times are simulated.
32 devices in a mesh: dp: 8 (over y, x, core), mp: 4 (over z).
Axes of the slice: x: 2, y: 2, z: 4, core: 2. Of those that a mesh axis runs over, the one named last changes fastest.
Arguments:
- query_heads: bfloat16 [4096, 3072], P('dp', 'mp'), may hold values from -48 to 48
- key_heads: bfloat16 [4096, 3072], P('dp', 'mp'), may hold values from -8 to 8
- value_heads: bfloat16 [4096, 3072], P('dp', 'mp'), may hold values from -6 to 6
- upstream: bfloat16 [4096, 3072], P('dp', 'mp'), may hold values from -6 to 6
- out_weight: bfloat16 [3072, 3072], P('dp', 'mp'), may hold values from -0.109375 to 0.109375
Outputs:
- grad_query: bfloat16 [4096, 3072], P('dp', 'mp')
- grad_key: bfloat16 [4096, 3072], P('dp', 'mp')
- grad_value: bfloat16 [4096, 3072], P('dp', 'mp')
- grad_weight: float32 [3072, 3072], P('dp', 'mp')
All inputs are finite; a program needn't handle non-finite values.
Results may differ from a plain program's by a relative error of at most 0.006.
Values may be sent and summed in bfloat16 or wider, within the bound.
A program may use at most 64 MiB of HBM per device.

v0:
```python
import jax
import jax.numpy as jnp
from jax import lax
from jax.sharding import PartitionSpec as P

HEAD = 128
PATCHES = 256


def shards(query_heads, key_heads, value_heads, upstream, out_weight):
    tokens_here = query_heads.shape[0]
    local_width = query_heads.shape[1]
    upstream_full = lax.all_gather(upstream, "mp", axis=1, tiled=True)
    columns = upstream_full
    context_sum = jnp.dot(
        columns,
        lax.all_gather(out_weight, "dp", axis=0, tiled=True),
        preferred_element_type=jnp.float32,
    )
    grad_context = context_sum.astype(jnp.bfloat16)
    images_here = tokens_here // PATCHES
    scaling = HEAD ** (-0.5)

    def heads_of(tensor):
        return tensor.reshape(images_here, PATCHES, -1, HEAD)

    def rows_of(tensor):
        return tensor.reshape(tokens_here, local_width).astype(jnp.bfloat16)

    query_split = heads_of(query_heads)
    key_split = heads_of(key_heads)
    value_split = heads_of(value_heads)
    context_split = heads_of(grad_context)
    scores = (
        jnp.einsum("bqhd,bkhd->bhqk", query_split, key_split, preferred_element_type=jnp.float32)
        * scaling
    )
    attention = jax.nn.softmax(scores, axis=-1)
    weights_bf = attention.astype(jnp.bfloat16)
    context = rows_of(
        jnp.einsum("bhqk,bkhd->bqhd", weights_bf, value_split, preferred_element_type=jnp.float32)
    )
    columns = upstream_full
    grad_weight = lax.psum_scatter(
        lax.dot_general(
            columns, context, (((0,), (0,)), ((), ())), preferred_element_type=jnp.float32
        ),
        "dp",
        scatter_dimension=0,
        tiled=True,
    )
    grad_value = rows_of(
        jnp.einsum("bhqk,bqhd->bkhd", weights_bf, context_split, preferred_element_type=jnp.float32)
    )
    grad_attention = jnp.einsum(
        "bqhd,bkhd->bhqk", context_split, value_split, preferred_element_type=jnp.float32
    )
    centred = jnp.sum(attention * grad_attention, axis=-1, keepdims=True)
    grad_scores = (attention * (grad_attention - centred) * scaling).astype(jnp.bfloat16)
    grad_query = rows_of(
        jnp.einsum("bhqk,bkhd->bqhd", grad_scores, key_split, preferred_element_type=jnp.float32)
    )
    grad_key = rows_of(
        jnp.einsum("bhqk,bqhd->bkhd", grad_scores, query_split, preferred_element_type=jnp.float32)
    )
    return (grad_query, grad_key, grad_value, grad_weight)


def solution(mesh):
    return jax.shard_map(
        shards,
        mesh=mesh,
        in_specs=(P("dp", "mp"), P("dp", "mp"), P("dp", "mp"), P("dp", "mp"), P("dp", "mp")),
        out_specs=(P("dp", "mp"), P("dp", "mp"), P("dp", "mp"), P("dp", "mp")),
        check_vma=False,
    )
```

profile of v0, /device:TPU:0, one launch (start us, length us, event | category | flops | bytes accessed | tf_op | source)
XLA Modules:
  0.0 204.6 jit_solution(11055972676345704808)
XLA Ops:
  7.2 0.0 all-gather.3.cloned.1.call-start
  7.2 0.7 all-gather.3.cloned.1.call-update
  7.9 0.0 all-gather.5.cloned.1.call-start
  8.0 0.7 all-gather.5.cloned.1.call-update
  8.7 0.0 reduce-scatter.2.cloned.1.call-start
  8.7 2.0 reshape.38
  10.7 0.9 reshape.39
  11.6 2.0 reshape.40
  13.6 0.6 fusion.37
  14.2 2.5 %fusion.46 = (f32[2,6,256]{2,1,0:T(8,128)S(1)}, f32[2,6,256,256]{2,3,1,0:T(8,128)S(1)}) fusion(f32[2,6,256,256]{2,3,1,0:T(8,128)S(1)} %fusion.37), kind=kOutput, calls=%fused_computation.42 | output fusion | flops 3145983 | bytes 6303744 | tf_op jit(solution)/shard_map/sub | solution.py:38
  16.7 1.6 copy-done.2
  18.3 1.6 fusion.30
  19.9 2.3 %copy.39 = bf16[2,256,6,128]{1,0,3,2:T(2,128)(2,1)S(1)} copy(bf16[2,256,6,128]{3,1,2,0:T(8,128)(2,1)} %fusion.30) | data formatting | bytes 1572864 | tf_op jit(solution)/shard_map/convert_element_type | solution.py:28
  22.3 1.1 copy.64
  23.3 52.5 %all-gather.3.cloned.1.call-done = bf16[512,3072]{1,0:T(8,128)(2,1)} async-done(((bf16[512,768]{1,0:T(8,128)(2,1)}), bf16[512,3072]{1,0:T(8,128)(2,1)}) %all-gather.3.cloned.1.call-update) | async-done | bytes 3145744 | tf_op jit(solution)/shard_map/all_gather | solution.py:13
  75.8 8.4 %convolution_bitcast_fusion = f32[3072,768]{0,1:T(8,128)} fusion(bf16[512,768]{0,1:T(8,128)(2,1)} %bitcast.39, bf16[512,3072]{1,0:T(8,128)(2,1)} %all-gather.3.cloned.1.call-done), kind=kOutput, calls=%fused_computation.2 | convolution fusion | flops 2415919104 | bytes 13369344 | tf_op jit(solution)/shard_map/dot_general | solution.py:45
  84.1 0.0 reduce-scatter.2.cloned.1.call-update
  84.2 31.2 %all-gather.5.cloned.1.call-done = bf16[3072,768]{1,0:T(8,128)(2,1)} async-done(((bf16[384,768]{1,0:T(8,128)(2,1)}), bf16[3072,768]{1,0:T(8,128)(2,1)}) %all-gather.5.cloned.1.call-update) | async-done | bytes 4718608 | tf_op jit(solution)/shard_map/all_gather | solution.py:17
  115.3 6.8 %convolution_convert_fusion.2 = bf16[512,768]{1,0:T(8,128)(2,1)} fusion(bf16[512,3072]{1,0:T(8,128)(2,1)} %all-gather.3.cloned.1.call-done, bf16[3072,768]{1,0:T(8,128)(2,1)} %all-gather.5.cloned.1.call-done), kind=kOutput, calls=%fused_computation.17 | convolution fusion | flops 2416312320 | bytes 8650752 | tf_op jit(solution)/shard_map/dot_general | solution.py:15
  122.1 2.0 reshape.41
  124.1 1.3 copy.34
  125.4 3.9 %fusion.34 = f32[2,6,256,256]{2,3,1,0:T(8,128)} fusion(bf16[2,256,6,128]{1,3,2,0:T(8,128)(2,1)} %copy.34, bf16[2,256,6,128]{3,2,1,0:T(8,128)(2,1)} %copy-done), kind=kOutput, calls=%fused_computation.30 | convolution fusion | flops 201326592 | bytes 4718592 | tf_op jit(solution)/shard_map/bqhd,bkhd->bhqk/dot_general | solution.py:55
  129.3 8.9 %fusion.23 = bf16[2,256,6,128]{3,1,2,0:T(8,128)(2,1)} fusion(f32[2,6,256,256]{2,3,1,0:T(8,128)} %fusion.34, bf16[2,256,6,128]{3,2,1,0:T(8,128)(2,1)S(1)} %reshape.38, f32[2,6,256,256]{2,3,1,0:T(8,128)} %copy-done.2, f32[2,6,256]{2,1,0:T(8,128)S(1)} %get-tuple-element.12), kind=kOutput, calls=%fused_computation.20 | convolution fusion | flops 207228160 | bytes 7876608 | tf_op jit(solution)/shard_map/bhqk,bqhd->bkhd/dot_general | solution.py:64
  138.3 1.7 copy.48
  140.0 3.4 %fusion.29 = bf16[2,256,6,128]{1,3,2,0:T(8,128)(2,1)} fusion(bf16[2,256,6,128]{1,3,2,0:T(8,128)(2,1)S(1)} %copy-done.1, f32[2,6,256,256]{2,3,1,0:T(8,128)} %copy-done.2, f32[2,6,256]{2,1,0:T(8,128)S(1)} %get-tuple-element.12), kind=kOutput, calls=%fused_computation.22 | convolution fusion | flops 203292672 | bytes 4730880 | tf_op jit(solution)/shard_map/bhqk,bqhd->bkhd/dot_general | solution.py:53
  143.4 1.7 copy.49
  145.1 7.0 %fusion.26 = bf16[2,256,6,128]{3,1,2,0:T(8,128)(2,1)} fusion(f32[2,6,256,256]{2,3,1,0:T(8,128)} %fusion.34, bf16[2,256,6,128]{3,2,1,0:T(8,128)(2,1)S(1)} %reshape.39, f32[2,6,256,256]{2,3,1,0:T(8,128)} %copy-done.2, f32[2,6,256]{2,1,0:T(8,128)S(1)} %get-tuple-element.12), kind=kOutput, calls=%fused_computation.21 | convolution fusion | flops 207228160 | bytes 7876608 | tf_op jit(solution)/shard_map/bhqk,bkhd->bqhd/dot_general | solution.py:61
  152.1 1.7 copy.47
  153.8 1.0 copy.80
  154.8 1.5 copy_bitcast_fusion
  156.3 39.1 %reduce-scatter.2.cloned.1.call-done = f32[384,768]{0,1:T(8,128)} async-done(((f32[3072,768]{0,1:T(8,128)}), f32[384,768]{0,1:T(8,128)}) %reduce-scatter.2.cloned.1.call-update) | async-done | bytes 1179664 | tf_op jit(solution)/shard_map/reduce_scatter | solution.py:44
  195.4 2.7 %copy.43 = f32[384,768]{1,0:T(8,128)} copy(f32[384,768]{0,1:T(8,128)} %reduce-scatter.2.cloned.1.call-done) | data formatting | bytes 2359296
  (7 shorter events, 0.0 us)
Async XLA Ops:
  7.2 3.5 %copy-start.3 = (bf16[512,768]{1,0:T(8,128)(2,1)S(1)}, bf16[512,768]{1,0:T(8,128)(2,1)}, u32[]{:S(2)}) copy-start(bf16[512,768]{1,0:T(8,128)(2,1)} %param.6) | copy-start | bytes 2359300
  7.2 68.6 %all-gather.3.cloned.1.call-start = ((), (), s32[]{:S(2)}) async-start(), calls=%async_computation.1 | async-start | bytes 3932160 | tf_op jit(solution)/shard_map/all_gather | solution.py:13
  7.9 107.4 %all-gather.5.cloned.1.call-start = ((), (), s32[]{:S(2)}) async-start(), calls=%async_computation.2 | async-start | bytes 5308416 | tf_op jit(solution)/shard_map/all_gather | solution.py:17
  8.7 186.7 %reduce-scatter.2.cloned.1.call-start = ((), (), s32[]{:S(2)}) async-start(), calls=%async_computation.3 | async-start | bytes 10616832 | tf_op jit(solution)/shard_map/reduce_scatter | solution.py:44
  13.6 3.1 %copy-start = (bf16[2,256,6,128]{3,2,1,0:T(8,128)(2,1)}, bf16[2,256,6,128]{3,2,1,0:T(8,128)(2,1)S(1)}, u32[]{:S(2)}) copy-start(bf16[2,256,6,128]{3,2,1,0:T(8,128)(2,1)S(1)} %reshape.40) | copy-start | bytes 2359300
  16.6 1.6 copy-start.2
  129.3 10.6 %copy-start.1 = (bf16[2,256,6,128]{1,3,2,0:T(8,128)(2,1)S(1)}, bf16[2,256,6,128]{1,3,2,0:T(8,128)(2,1)}, u32[]{:S(2)}) copy-start(bf16[2,256,6,128]{1,3,2,0:T(8,128)(2,1)} %copy.34) | copy-start | bytes 2359300
Sparse Core Ops, SparseCore 0:
  9.6 66.1 all-gather.2
  77.7 37.6 all-gather.4
  118.9 76.4 reduce-scatter.1
where the time goes:
time: 205 us
  waiting for transfers between devices  124 us (60%)
  matrix products  40.7 us (20%)
  local copies, waits for them, and re-layouts  23.3 us (11%)
  between operations  13.9 us (7%)
  other arithmetic  2.47 us (1%)
    all_gather x1, waiting for transfers between devices, shards(): upstream_full = lax.all_gather(upstream, 'mp', axis=1, tiled=True)  52.5 us
    reduce_scatter x1, waiting for transfers between devices, shards(): lax.psum_scatter(lax.dot_general(columns, context, (((0,), (0,)), ((), ()...  39.1 us
    all_gather x1, waiting for transfers between devices, shards(): lax.all_gather(out_weight, 'dp', axis=0, tiled=True)  31.2 us
    unnamed x15, local copies, waits for them, and re-layouts  12.8 us
    dot_general x1, matrix products, shards(): jnp.einsum('bhqk,bqhd->bkhd', grad_scores, query_split, preferred_element...  8.95 us
    dot_general x1, matrix products, shards(): lax.dot_general(columns, context, (((0,), (0,)), ((), ())), preferred_ele...  8.37 us
    reshape x5, local copies, waits for them, and re-layouts, heads_of(): return tensor.reshape(images_here, PATCHES, -1, HEAD)  8.14 us
    dot_general x1, matrix products, shards(): jnp.einsum('bhqk,bkhd->bqhd', grad_scores, key_split, preferred_element_t...  7.04 us
  transfers between devices with their start and end apart: 3, of which 3 were waited for; matrix products, arithmetic and copies ran while one was open for 30% of the time, Pallas kernels for 0%

commit v1 on v0

--- a/solution.py
+++ b/solution.py
@@ -1,6 +1,8 @@
 import jax
 import jax.numpy as jnp
 from jax import lax
+from jax.experimental import pallas as pl
+from jax.experimental.pallas import tpu as pltpu
 from jax.sharding import PartitionSpec as P
 
 HEAD = 128
@@ -66,9 +68,313 @@
     return (grad_query, grad_key, grad_value, grad_weight)
 
 
+MESH = pl.DeviceIdType.MESH
+PLANES = 4
+CHIPS = 4
+PIECES = 3
+PIECE = 128
+
+
+def dot(left, right, left_dim, right_dim):
+    return lax.dot_general(
+        left, right, (((left_dim,), (right_dim,)), ((), ())), preferred_element_type=jnp.float32
+    )
+
+
+def fused_kernel(
+    q_ref, k_ref, v_ref, u_ref, w_ref,
+    gq_ref, gk_ref, gv_ref, gw_ref,
+    u_all, w_all, attention, context, grad_context, partial, pair_out, pair_in, sum_out, sum_in,
+    up_send, down_send, u_recv, pair_send, pair_recv, sum_send, sum_recv, w_send, w_recv,
+):
+    rank = lax.axis_index("dp")
+    plane = lax.axis_index("mp")
+    chip, core = rank // 2, rank % 2
+    sibling = rank + 1 - 2 * core
+    tokens, width = q_ref.shape
+    heads = width // HEAD
+    images = tokens // PATCHES
+    scaling = HEAD ** (-0.5)
+    chips_at = (chip, chip + 1 - 2 * (chip % 2), chip + 2 - 4 * (chip // 2), 3 - chip)
+
+    def at(rank_there, plane_there):
+        return {"dp": rank_there, "mp": plane_there}
+
+    barrier = pltpu.get_barrier_semaphore()
+    for rank_there in (sibling,) + tuple(2 * other + core for other in chips_at[1:]):
+        pl.semaphore_signal(barrier, inc=1, device_id=at(rank_there, plane), device_id_type=MESH)
+    for plane_there in ((plane + 1) % PLANES, (plane + PLANES - 1) % PLANES):
+        pl.semaphore_signal(barrier, inc=1, device_id=at(rank, plane_there), device_id_type=MESH)
+
+    for piece in range(PIECES):
+        for half in range(2):
+            u_all[plane, piece, :, half * PIECE : (half + 1) * PIECE] = u_ref[
+                :, (half * PIECES + piece) * PIECE : (half * PIECES + piece + 1) * PIECE
+            ]
+
+    pl.semaphore_wait(barrier, 6)
+
+    def remote(src, dst, send, recv, rank_there, plane_there):
+        return pltpu.make_async_remote_copy(
+            src_ref=src, dst_ref=dst, send_sem=send, recv_sem=recv,
+            device_id=at(rank_there, plane_there), device_id_type=MESH,
+        )
+
+    def up_copy(shard, piece):
+        block = u_all.at[shard, piece]
+        return remote(
+            block, block, up_send.at[shard, piece], u_recv.at[shard, piece], rank,
+            (plane + 1) % PLANES,
+        )
+
+    def down_copy(shard, piece):
+        block = u_all.at[shard, piece]
+        return remote(
+            block, block, down_send.at[shard, piece], u_recv.at[shard, piece], rank,
+            (plane + PLANES - 1) % PLANES,
+        )
+
+    def goes_up(shard):
+        return (plane < PLANES - 1) & (shard <= plane)
+
+    def goes_down(shard):
+        return (plane > 0) & (shard >= plane)
+
+    def send_on(shard, piece):
+        @pl.when(goes_up(shard))
+        def _():
+            up_copy(shard, piece).start()
+
+        @pl.when(goes_down(shard))
+        def _():
+            down_copy(shard, piece).start()
+
+    send_on(plane, 0)
+
+    def w_copy(step):
+        if step == 0:
+            return remote(
+                w_ref, w_all.at[chip, :, core], w_send.at[0], w_recv.at[0], sibling, plane
+            )
+        return remote(
+            w_ref, w_all.at[chip, :, core], w_send.at[step], w_recv.at[step],
+            2 * chips_at[step] + core, plane,
+        )
+
+    def w_forward(step):
+        block = w_all.at[chips_at[step], :, core]
+        return remote(block, block, w_send.at[3 + step], w_recv.at[3 + step], sibling, plane)
+
+    for step in (1, 2, 3, 0):
+        w_copy(step).start()
+    send_on(plane, 1)
+    for piece in range(PIECES):
+        w_all[chip, piece, core] = w_ref[piece]
+
+    def rows_columns(index):
+        rows = pl.ds(pl.multiple_of((index // heads) * PATCHES, PATCHES), PATCHES)
+        columns = pl.ds(pl.multiple_of((index % heads) * HEAD, HEAD), HEAD)
+        return rows, columns
+
+    def forward(index, carry):
+        rows, columns = rows_columns(index)
+        scores = dot(q_ref[rows, columns], k_ref[rows, columns], 1, 1) * scaling
+        raised = jnp.exp(scores - jnp.max(scores, axis=-1, keepdims=True))
+        weights = raised / jnp.sum(raised, axis=-1, keepdims=True)
+        attention[index] = weights
+        context[rows, columns] = dot(
+            weights.astype(jnp.bfloat16), v_ref[rows, columns], 1, 0
+        ).astype(jnp.bfloat16)
+        return carry
+
+    lax.fori_loop(0, images * heads, forward, 0)
+    grad_context[...] = jnp.zeros_like(grad_context)
+
+    def pair_copy(shard, piece):
+        return remote(
+            pair_out.at[shard, piece], pair_in.at[shard, piece], pair_send.at[shard, piece],
+            pair_recv.at[shard, piece], sibling, plane,
+        )
+
+    def sum_copy(shard, piece):
+        return remote(
+            sum_out.at[shard, piece], sum_in.at[chip, piece], sum_send.at[shard, piece],
+            sum_recv.at[chip, piece], 2 * shard + core, plane,
+        )
+
+    def shard_of(order):
+        distance = (order + 1) // 2
+        shard = plane + distance * (1 - 2 * (order % 2))
+        return shard, (shard >= 0) & (shard < PLANES)
+
+    def finish(order, piece):
+        shard, valid = shard_of(order)
+
+        @pl.when(valid)
+        def _():
+            pair_copy(shard, piece).wait_recv()
+
+            @pl.when(shard == chip)
+            def _():
+                partial[shard, piece, core] += pair_in[shard, piece].astype(jnp.float32)
+
+            @pl.when(shard != chip)
+            def _():
+                total = partial[shard, piece, core] + pair_in[shard, piece].astype(jnp.float32)
+                sum_out[shard, piece] = total.astype(jnp.bfloat16)
+                sum_copy(shard, piece).start()
+
+    def visit(order, piece, last):
+        shard, valid = shard_of(order)
+
+        @pl.when(valid)
+        def _():
+            @pl.when(order > 0)
+            def _():
+                up_copy(shard, piece).wait_recv()
+                send_on(shard, piece)
+
+        @pl.when(order > 0)
+        def _():
+            finish(order - 1, piece)
+
+        @pl.when(valid)
+        def _():
+            for tile in range(width // 256):
+                columns = slice(tile * 256, (tile + 1) * 256)
+                product = dot(u_all[shard, piece], context[:, columns], 0, 0)
+                partial[shard, piece, :, :, columns] = product.reshape(2, PIECE, 256)
+            pair_out[shard, piece] = partial[shard, piece, 1 - core].astype(jnp.bfloat16)
+            pair_copy(shard, piece).start()
+            if last:
+                def tile_of(tile, carry):
+                    columns = pl.ds(pl.multiple_of(tile * 256, 256), 256)
+                    total = grad_context[:, columns]
+                    for part in range(PIECES):
+                        rows = w_all[shard, part, :, :, columns].reshape(2 * PIECE, 256)
+                        total += dot(u_all[shard, part], rows, 1, 0)
+                    grad_context[:, columns] = total
+                    return carry
+
+                lax.fori_loop(0, width // 256, tile_of, 0)
+
+    orders = 2 * PLANES - 1
+    for piece in range(PIECES):
+        if piece == PIECES - 1:
+            for step in (1, 2, 3):
+                w_copy(step).wait_recv()
+                w_forward(step).start()
+            w_copy(0).wait_recv()
+            for step in (1, 2, 3):
+                w_forward(step).wait_recv()
+
+        def step_of(order, carry, piece=piece):
+            visit(order, piece, piece == PIECES - 1)
+            return carry
+
+        lax.fori_loop(0, orders, step_of, 0)
+        if piece + 2 < PIECES:
+            send_on(plane, piece + 2)
+        finish(orders - 1, piece)
+
+    def backward(index, carry):
+        rows, columns = rows_columns(index)
+        weights = attention[index]
+        weights_bf = weights.astype(jnp.bfloat16)
+        context_grad = grad_context[rows, columns].astype(jnp.bfloat16)
+        gv_ref[rows, columns] = dot(weights_bf, context_grad, 0, 0).astype(jnp.bfloat16)
+        attention_grad = dot(context_grad, v_ref[rows, columns], 1, 1)
+        centred = jnp.sum(weights * attention_grad, axis=-1, keepdims=True)
+        scores_grad = (weights * (attention_grad - centred) * scaling).astype(jnp.bfloat16)
+        gq_ref[rows, columns] = dot(scores_grad, k_ref[rows, columns], 1, 0).astype(jnp.bfloat16)
+        gk_ref[rows, columns] = dot(scores_grad, q_ref[rows, columns], 0, 0).astype(jnp.bfloat16)
+        return carry
+
+    lax.fori_loop(0, images * heads, backward, 0)
+
+    for piece in range(PIECES):
+        total = partial[chip, piece, core]
+        for other in chips_at[1:]:
+            block = sum_in.at[other, piece]
+            remote(
+                block, block, sum_send.at[other, piece], sum_recv.at[other, piece],
+                2 * other + core, plane,
+            ).wait_recv()
+            total += sum_in[other, piece].astype(jnp.float32)
+        gw_ref[piece * PIECE : (piece + 1) * PIECE, :] = total
+
+    for step in range(4):
+        w_copy(step).wait_send()
+        if step:
+            w_forward(step).wait_send()
+
+    def drain(index, carry):
+        shard, piece = index // PIECES, index % PIECES
+        pair_copy(shard, piece).wait_send()
+
+        @pl.when(shard != chip)
+        def _():
+            sum_copy(shard, piece).wait_send()
+
+        @pl.when(goes_up(shard))
+        def _():
+            up_copy(shard, piece).wait_send()
+
+        @pl.when(goes_down(shard))
+        def _():
+            down_copy(shard, piece).wait_send()
+
+        return carry
+
+    lax.fori_loop(0, PLANES * PIECES, drain, 0)
+
+
+def fused_shards(query_heads, key_heads, value_heads, upstream, out_weight):
+    tokens, width = query_heads.shape
+    rows = out_weight.shape[0]
+    heads = (tokens // PATCHES) * (width // HEAD)
+    bf16, f32 = jnp.bfloat16, jnp.float32
+    many = pltpu.SemaphoreType.DMA((PLANES, PIECES))
+    few = pltpu.SemaphoreType.DMA((7,))
+    piece_of = (PLANES, PIECES, PIECE, width)
+    vmem = pl.BlockSpec(memory_space=pltpu.VMEM)
+    return pl.pallas_call(
+        fused_kernel,
+        out_shape=[jax.ShapeDtypeStruct((tokens, width), bf16)] * 3
+        + [jax.ShapeDtypeStruct((rows, width), f32)],
+        in_specs=[vmem] * 5,
+        out_specs=[vmem] * 4,
+        scratch_shapes=[
+            pltpu.VMEM((PLANES, PIECES, tokens, 2 * PIECE), bf16),
+            pltpu.VMEM((CHIPS, PIECES, 2, PIECE, width), bf16),
+            pltpu.VMEM((heads, PATCHES, PATCHES), f32),
+            pltpu.VMEM((tokens, width), bf16),
+            pltpu.VMEM((tokens, width), f32),
+            pltpu.VMEM((PLANES, PIECES, 2, PIECE, width), f32),
+            pltpu.VMEM(piece_of, bf16),
+            pltpu.VMEM(piece_of, bf16),
+            pltpu.VMEM(piece_of, bf16),
+            pltpu.VMEM(piece_of, bf16),
+        ]
+        + [many] * 7
+        + [few] * 2,
+        compiler_params=pltpu.CompilerParams(
+            collective_id=0, has_side_effects=True, vmem_limit_bytes=56 * 2**20
+        ),
+        cost_estimate=pl.CostEstimate(
+            flops=6_000_000_000, bytes_accessed=8_000_000, transcendentals=786_432
+        ),
+        name="fused",
+    )(
+        query_heads, key_heads, value_heads, upstream,
+        out_weight.reshape(PIECES, PIECE, width),
+    )
+
+
 def solution(mesh):
+    fits = mesh.shape["dp"] == 2 * CHIPS and mesh.shape["mp"] == PLANES
     return jax.shard_map(
-        shards,
+        fused_shards if fits else shards,
         mesh=mesh,
         in_specs=(P("dp", "mp"), P("dp", "mp"), P("dp", "mp"), P("dp", "mp"), P("dp", "mp")),
         out_specs=(P("dp", "mp"), P("dp", "mp"), P("dp", "mp"), P("dp", "mp")),

time: 205 us -> 82.5 us (0.40)
  waiting for transfers between devices: 124 us -> 0 us
  Pallas kernels: 0 us -> 74.7 us
  matrix products: 40.7 us -> 0 us
  local copies, waits for them, and re-layouts: 23.3 us -> 6.12 us
  between operations: 13.9 us -> 0.65 us
  other arithmetic: 2.47 us -> 0 us
    all_gather x2 -> x0, waiting for transfers between devices: 83.6 us -> none  [the longest x1 52.5 us: shards(): upstream_full = lax.all_gather(upstream, 'mp', axis=1, tiled=True)]
    pallas_call x0 -> x1, Pallas kernels: none -> 74.7 us  [fused_shards(): pl.pallas_call(fused_kernel, out_shape=[jax.ShapeDtypeStruct((tokens, wid...]
    dot_general x8 -> x0, matrix products: 40.7 us -> none  [the longest x1 8.95 us: shards(): jnp.einsum('bhqk,bqhd->bkhd', grad_scores, query_split, preferred_element...]
    reduce_scatter x1 -> x0, waiting for transfers between devices: 39.1 us -> none  [shards(): lax.psum_scatter(lax.dot_general(columns, context, (((0,), (0,)), ((), ()...]
    reshape x5 -> x0, local copies, waits for them, and re-layouts: 8.14 us -> none  [heads_of(): return tensor.reshape(images_here, PATCHES, -1, HEAD)]
    unnamed x15 -> x10, local copies, waits for them, and re-layouts: 12.8 us -> 6.12 us
    sub x1 -> x0, other arithmetic: 2.47 us -> none  [shards(): attention = jax.nn.softmax(scores, axis=-1)]
    convert_element_type x1 -> x0, local copies, waits for them, and re-layouts: 2.34 us -> none  [rows_of(): return tensor.reshape(tokens_here, local_width).astype(jnp.bfloat16)]
  transfers between devices with their start and end apart: 3 -> 0, of which waited for: 3 -> 0; matrix products, arithmetic and copies ran while one was open for 30% -> 0% of each run, Pallas kernels for 0% -> 0%
where the time goes in v1:
time: 82.5 us; the launch traced here: 81.5 us
  Pallas kernels  74.7 us (91%)
  local copies, waits for them, and re-layouts  6.12 us (7%)
    pallas_call x1, Pallas kernels, fused_shards(): pl.pallas_call(fused_kernel, out_shape=[jax.ShapeDtypeStruct((tokens, wid...  74.7 us
    unnamed x10, local copies, waits for them, and re-layouts  6.12 us

profile of v1, /device:TPU:0, one launch (start us, length us, event | category | flops | bytes accessed | tf_op | source)
XLA Modules:
  0.0 81.5 jit_solution(7243633483370142404)
XLA Ops:
  0.6 74.7 %fused.1 = (bf16[512,768]{1,0:T(8,128)(2,1)}, bf16[512,768]{1,0:T(8,128)(2,1)}, bf16[512,768]{1,0:T(8,128)(2,1)}, f32[384,768]{1,0:T(8,128)}) custom-call(bf16[512,768]{1,0:T(8,128)(2,1)} %q_ref.1, bf16[512,768]{1,0:T(8,128)(2,1)} %k_ref.1, bf16[512,768]{1,0:T(8,128)(2,1)} %v_ref.1, bf16[512,768]{1,0:T(8,128)(2,1)} %u_ref.1, bf16[3,128,768]{2,1,0:T(8,128)(2,1)} %bitcast.1), custom_call_target="tpu_custom_call" | custom-call | flops 6000000000 | bytes 8000000 | tf_op jit(solution)/shard_map/fused/pallas_call | solution.py:341
  75.4 0.0 copy-start.2
  75.4 2.1 %copy.13 = bf16[512,768]{1,0:T(8,128)(2,1)} copy(bf16[512,768]{1,0:T(8,128)(2,1)} %get-tuple-element.8) | data formatting | bytes 1572864
  77.5 0.0 copy-done.2
  77.5 0.0 copy-start.1
  77.5 0.9 %copy.14 = bf16[512,768]{1,0:T(8,128)(2,1)} copy(bf16[512,768]{1,0:T(8,128)(2,1)S(1)} %copy-done.2) | data formatting | bytes 1572864
  78.4 0.5 copy-done.1
  78.9 0.0 copy-start
  78.9 0.9 %copy.15 = bf16[512,768]{1,0:T(8,128)(2,1)} copy(bf16[512,768]{1,0:T(8,128)(2,1)S(1)} %copy-done.1) | data formatting | bytes 1572864
  79.8 0.7 copy-done
  80.5 1.0 %copy.16 = f32[384,768]{1,0:T(8,128)} copy(f32[384,768]{1,0:T(8,128)S(1)} %copy-done) | data formatting | bytes 2359296
Async XLA Ops:
  75.4 2.1 %copy-start.2 = (bf16[512,768]{1,0:T(8,128)(2,1)S(1)}, bf16[512,768]{1,0:T(8,128)(2,1)}, u32[]{:S(2)}) copy-start(bf16[512,768]{1,0:T(8,128)(2,1)} %get-tuple-element.9) | copy-start | bytes 2359300
  77.5 1.4 %copy-start.1 = (bf16[512,768]{1,0:T(8,128)(2,1)S(1)}, bf16[512,768]{1,0:T(8,128)(2,1)}, u32[]{:S(2)}) copy-start(bf16[512,768]{1,0:T(8,128)(2,1)} %get-tuple-element.10) | copy-start | bytes 2359300
  78.9 1.6 %copy-start = (f32[384,768]{1,0:T(8,128)S(1)}, f32[384,768]{1,0:T(8,128)}, u32[]{:S(2)}) copy-start(f32[384,768]{1,0:T(8,128)} %get-tuple-element.11) | copy-start | bytes 3538948

commit v2 on v1

--- a/solution.py
+++ b/solution.py
@@ -82,10 +82,11 @@
 
 
 def fused_kernel(
-    q_ref, k_ref, v_ref, u_ref, w_ref,
-    gq_ref, gk_ref, gv_ref, gw_ref,
+    q_hbm, k_hbm, v_hbm, u_hbm, w_hbm,
+    gq_hbm, gk_hbm, gv_hbm, gw_hbm,
+    q_ref, k_ref, v_ref, gq_ref, gk_ref, gv_ref, gw_ref,
     u_all, w_all, attention, context, grad_context, partial, pair_out, pair_in, sum_out, sum_in,
-    up_send, down_send, u_recv, pair_send, pair_recv, sum_send, sum_recv, w_send, w_recv,
+    up_send, down_send, u_recv, pair_send, pair_recv, sum_send, sum_recv, w_send, w_recv, u_load, load, store,
 ):
     rank = lax.axis_index("dp")
     plane = lax.axis_index("mp")
@@ -106,12 +107,27 @@
     for plane_there in ((plane + 1) % PLANES, (plane + PLANES - 1) % PLANES):
         pl.semaphore_signal(barrier, inc=1, device_id=at(rank, plane_there), device_id_type=MESH)
 
+    def u_loads(piece):
+        return [
+            pltpu.make_async_copy(
+                u_hbm.at[:, pl.ds((half * PIECES + piece) * PIECE, PIECE)],
+                u_all.at[plane, piece, :, pl.ds(half * PIECE, PIECE)],
+                u_load.at[piece, half],
+            )
+            for half in range(2)
+        ]
+
+    loads = [
+        pltpu.make_async_copy(q_hbm, q_ref, load.at[0]),
+        pltpu.make_async_copy(k_hbm, k_ref, load.at[1]),
+        pltpu.make_async_copy(v_hbm, v_ref, load.at[2]),
+        pltpu.make_async_copy(w_hbm, w_all.at[chip, :, core], load.at[3]),
+    ]
     for piece in range(PIECES):
-        for half in range(2):
-            u_all[plane, piece, :, half * PIECE : (half + 1) * PIECE] = u_ref[
-                :, (half * PIECES + piece) * PIECE : (half * PIECES + piece + 1) * PIECE
-            ]
-
+        for copy in u_loads(piece):
+            copy.start()
+    for copy in loads:
+        copy.start()
     pl.semaphore_wait(barrier, 6)
 
     def remote(src, dst, send, recv, rank_there, plane_there):
@@ -149,15 +165,17 @@
         def _():
             down_copy(shard, piece).start()
 
+    for copy in u_loads(0):
+        copy.wait()
     send_on(plane, 0)
 
     def w_copy(step):
         if step == 0:
             return remote(
-                w_ref, w_all.at[chip, :, core], w_send.at[0], w_recv.at[0], sibling, plane
+                w_hbm, w_all.at[chip, :, core], w_send.at[0], w_recv.at[0], sibling, plane
             )
         return remote(
-            w_ref, w_all.at[chip, :, core], w_send.at[step], w_recv.at[step],
+            w_hbm, w_all.at[chip, :, core], w_send.at[step], w_recv.at[step],
             2 * chips_at[step] + core, plane,
         )
 
@@ -167,9 +185,12 @@
 
     for step in (1, 2, 3, 0):
         w_copy(step).start()
-    send_on(plane, 1)
-    for piece in range(PIECES):
-        w_all[chip, piece, core] = w_ref[piece]
+    for piece in range(1, PIECES):
+        for copy in u_loads(piece):
+            copy.wait()
+        send_on(plane, piece)
+    for copy in loads:
+        copy.wait()
 
     def rows_columns(index):
         rows = pl.ds(pl.multiple_of((index // heads) * PATCHES, PATCHES), PATCHES)
@@ -273,8 +294,6 @@
             return carry
 
         lax.fori_loop(0, orders, step_of, 0)
-        if piece + 2 < PIECES:
-            send_on(plane, piece + 2)
         finish(orders - 1, piece)
 
     def backward(index, carry):
@@ -291,6 +310,14 @@
         return carry
 
     lax.fori_loop(0, images * heads, backward, 0)
+    stores = [
+        pltpu.make_async_copy(gq_ref, gq_hbm, store.at[0]),
+        pltpu.make_async_copy(gk_ref, gk_hbm, store.at[1]),
+        pltpu.make_async_copy(gv_ref, gv_hbm, store.at[2]),
+        pltpu.make_async_copy(gw_ref, gw_hbm, store.at[3]),
+    ]
+    for copy in stores[:3]:
+        copy.start()
 
     for piece in range(PIECES):
         total = partial[chip, piece, core]
@@ -302,6 +329,7 @@
             ).wait_recv()
             total += sum_in[other, piece].astype(jnp.float32)
         gw_ref[piece * PIECE : (piece + 1) * PIECE, :] = total
+    stores[3].start()
 
     for step in range(4):
         w_copy(step).wait_send()
@@ -327,6 +355,13 @@
         return carry
 
     lax.fori_loop(0, PLANES * PIECES, drain, 0)
+    for copy in stores:
+        copy.wait()
+
+
+def place_kernel(*refs):
+    for source, target in zip(refs[:4], refs[4:]):
+        target[...] = source[...]
 
 
 def fused_shards(query_heads, key_heads, value_heads, upstream, out_weight):
@@ -337,14 +372,17 @@
     many = pltpu.SemaphoreType.DMA((PLANES, PIECES))
     few = pltpu.SemaphoreType.DMA((7,))
     piece_of = (PLANES, PIECES, PIECE, width)
-    vmem = pl.BlockSpec(memory_space=pltpu.VMEM)
-    return pl.pallas_call(
+    hbm = pl.BlockSpec(memory_space=pltpu.HBM)
+    out_shape = [jax.ShapeDtypeStruct((tokens, width), bf16)] * 3
+    out_shape += [jax.ShapeDtypeStruct((rows, width), f32)]
+    grads = pl.pallas_call(
         fused_kernel,
-        out_shape=[jax.ShapeDtypeStruct((tokens, width), bf16)] * 3
-        + [jax.ShapeDtypeStruct((rows, width), f32)],
-        in_specs=[vmem] * 5,
-        out_specs=[vmem] * 4,
-        scratch_shapes=[
+        out_shape=out_shape,
+        in_specs=[hbm] * 5,
+        out_specs=[hbm] * 4,
+        scratch_shapes=[pltpu.VMEM((tokens, width), bf16)] * 6
+        + [pltpu.VMEM((rows, width), f32)]
+        + [
             pltpu.VMEM((PLANES, PIECES, tokens, 2 * PIECE), bf16),
             pltpu.VMEM((CHIPS, PIECES, 2, PIECE, width), bf16),
             pltpu.VMEM((heads, PATCHES, PATCHES), f32),
@@ -357,7 +395,12 @@
             pltpu.VMEM(piece_of, bf16),
         ]
         + [many] * 7
-        + [few] * 2,
+        + [few] * 2
+        + [
+            pltpu.SemaphoreType.DMA((PIECES, 2)),
+            pltpu.SemaphoreType.DMA((4,)),
+            pltpu.SemaphoreType.DMA((4,)),
+        ],
         compiler_params=pltpu.CompilerParams(
             collective_id=0, has_side_effects=True, vmem_limit_bytes=56 * 2**20
         ),
@@ -369,6 +412,17 @@
         query_heads, key_heads, value_heads, upstream,
         out_weight.reshape(PIECES, PIECE, width),
     )
+    steps = 2
+    blocks = [pl.BlockSpec((tokens // steps, width), lambda step: (step, 0))] * 3
+    blocks += [pl.BlockSpec((rows // steps, width), lambda step: (step, 0))]
+    return pl.pallas_call(
+        place_kernel,
+        grid=(steps,),
+        out_shape=out_shape,
+        in_specs=blocks,
+        out_specs=blocks,
+        name="place",
+    )(*grads)
 
 
 def solution(mesh):

time: 82.5 us -> 77.2 us (0.936)
  local copies, waits for them, and re-layouts: 6.12 us -> 0 us
  Pallas kernels: 74.7 us -> 75.9 us
    unnamed x10 -> x0, local copies, waits for them, and re-layouts: 6.12 us -> none
    pallas_call x1 -> x2, Pallas kernels: 74.7 us -> 75.9 us  [the longest x1 72.6 us: fused_shards(): pl.pallas_call(fused_kernel, out_shape=out_shape, in_specs=[hbm] * 5, out...]
where the time goes in v2:
time: 77.2 us; the launch traced here: 76.6 us
  Pallas kernels  75.9 us (98%)
    pallas_call x1, Pallas kernels, fused_shards(): pl.pallas_call(fused_kernel, out_shape=out_shape, in_specs=[hbm] * 5, out...  72.6 us
    pallas_call x1, Pallas kernels, fused_shards(): pl.pallas_call(place_kernel, grid=(steps,), out_shape=out_shape, in_specs...  3.34 us

profile of v2, /device:TPU:0, one launch (start us, length us, event | category | flops | bytes accessed | tf_op | source)
XLA Modules:
  0.0 76.6 jit_solution(5665031274970565737)
XLA Ops:
  0.6 72.6 %fused.1 = (bf16[512,768]{1,0:T(8,128)(2,1)}, bf16[512,768]{1,0:T(8,128)(2,1)}, bf16[512,768]{1,0:T(8,128)(2,1)}, f32[384,768]{1,0:T(8,128)}) custom-call(bf16[512,768]{1,0:T(8,128)(2,1)} %q_hbm.1, bf16[512,768]{1,0:T(8,128)(2,1)} %k_hbm.1, bf16[512,768]{1,0:T(8,128)(2,1)} %v_hbm.1, bf16[512,768]{1,0:T(8,128)(2,1)} %u_hbm.1, bf16[3,128,768]{2,1,0:T(8,128)(2,1)} %bitcast.1), custom_call_target="tpu_custom_call" | custom-call | flops 6000000000 | bytes 8000000 | tf_op jit(solution)/shard_map/fused/pallas_call | solution.py:378
  73.2 3.3 %place.1 = (bf16[512,768]{1,0:T(8,128)(2,1)}, bf16[512,768]{1,0:T(8,128)(2,1)}, bf16[512,768]{1,0:T(8,128)(2,1)}, f32[384,768]{1,0:T(8,128)}) custom-call(bf16[512,768]{1,0:T(8,128)(2,1)} %get-tuple-element.8.refs_0_, bf16[512,768]{1,0:T(8,128)(2,1)} %get-tuple-element.9.refs_1_, bf16[512,768]{1,0:T(8,128)(2,1)} %get-tuple-element.10.refs_2_, ...), custom_call_target="tpu_custom_call" | custom-call | tf_op jit(solution)/shard_map/place/pallas_call | solution.py:418

commit v3 on v2

--- a/solution.py
+++ b/solution.py
@@ -209,7 +209,6 @@
         return carry
 
     lax.fori_loop(0, images * heads, forward, 0)
-    grad_context[...] = jnp.zeros_like(grad_context)
 
     def pair_copy(shard, piece):
         return remote(
@@ -258,6 +257,13 @@
         @pl.when(order > 0)
         def _():
             finish(order - 1, piece)
+
+        if last:
+            @pl.when(order == 4)
+            def _():
+                for step in (1, 2, 3):
+                    w_copy(step).wait_recv()
+                    w_forward(step).start()
 
         @pl.when(valid)
         def _():
@@ -267,28 +273,9 @@
                 partial[shard, piece, :, :, columns] = product.reshape(2, PIECE, 256)
             pair_out[shard, piece] = partial[shard, piece, 1 - core].astype(jnp.bfloat16)
             pair_copy(shard, piece).start()
-            if last:
-                def tile_of(tile, carry):
-                    columns = pl.ds(pl.multiple_of(tile * 256, 256), 256)
-                    total = grad_context[:, columns]
-                    for part in range(PIECES):
-                        rows = w_all[shard, part, :, :, columns].reshape(2 * PIECE, 256)
-                        total += dot(u_all[shard, part], rows, 1, 0)
-                    grad_context[:, columns] = total
-                    return carry
-
-                lax.fori_loop(0, width // 256, tile_of, 0)
 
     orders = 2 * PLANES - 1
     for piece in range(PIECES):
-        if piece == PIECES - 1:
-            for step in (1, 2, 3):
-                w_copy(step).wait_recv()
-                w_forward(step).start()
-            w_copy(0).wait_recv()
-            for step in (1, 2, 3):
-                w_forward(step).wait_recv()
-
         def step_of(order, carry, piece=piece):
             visit(order, piece, piece == PIECES - 1)
             return carry
@@ -309,6 +296,21 @@
         gk_ref[rows, columns] = dot(scores_grad, q_ref[rows, columns], 0, 0).astype(jnp.bfloat16)
         return carry
 
+    w_copy(0).wait_recv()
+    for step in (1, 2, 3):
+        w_forward(step).wait_recv()
+
+    def project(tile, carry):
+        columns = pl.ds(pl.multiple_of(tile * 256, 256), 256)
+        total = jnp.zeros((tokens, 256), jnp.float32)
+        for shard in range(PLANES):
+            for part in range(PIECES):
+                rows = w_all[shard, part, :, :, columns].reshape(2 * PIECE, 256)
+                total += dot(u_all[shard, part], rows, 1, 0)
+        grad_context[:, columns] = total
+        return carry
+
+    lax.fori_loop(0, width // 256, project, 0)
     lax.fori_loop(0, images * heads, backward, 0)
     stores = [
         pltpu.make_async_copy(gq_ref, gq_hbm, store.at[0]),

time: 77.2 us -> 75.8 us (0.982)
  Pallas kernels: 75.9 us -> 74.6 us
    pallas_call x1, Pallas kernels: 72.6 us -> 71.3 us  [fused_shards(): pl.pallas_call(fused_kernel, out_shape=out_shape, in_specs=[hbm] * 5, out...]
where the time goes in v3:
time: 75.8 us; the launch traced here: 75.3 us
  Pallas kernels  74.6 us (98%)
    pallas_call x1, Pallas kernels, fused_shards(): pl.pallas_call(fused_kernel, out_shape=out_shape, in_specs=[hbm] * 5, out...  71.3 us
    pallas_call x1, Pallas kernels, fused_shards(): pl.pallas_call(place_kernel, grid=(steps,), out_shape=out_shape, in_specs...  3.34 us

profile of v3, /device:TPU:0, one launch (start us, length us, event | category | flops | bytes accessed | tf_op | source)
XLA Modules:
  0.0 75.3 jit_solution(9430649601979890750)
XLA Ops:
  0.6 71.3 %fused.1 = (bf16[512,768]{1,0:T(8,128)(2,1)}, bf16[512,768]{1,0:T(8,128)(2,1)}, bf16[512,768]{1,0:T(8,128)(2,1)}, f32[384,768]{1,0:T(8,128)}) custom-call(bf16[512,768]{1,0:T(8,128)(2,1)} %q_hbm.1, bf16[512,768]{1,0:T(8,128)(2,1)} %k_hbm.1, bf16[512,768]{1,0:T(8,128)(2,1)} %v_hbm.1, bf16[512,768]{1,0:T(8,128)(2,1)} %u_hbm.1, bf16[3,128,768]{2,1,0:T(8,128)(2,1)} %bitcast.1), custom_call_target="tpu_custom_call" | custom-call | flops 6000000000 | bytes 8000000 | tf_op jit(solution)/shard_map/fused/pallas_call | solution.py:380
  71.9 3.3 %place.1 = (bf16[512,768]{1,0:T(8,128)(2,1)}, bf16[512,768]{1,0:T(8,128)(2,1)}, bf16[512,768]{1,0:T(8,128)(2,1)}, f32[384,768]{1,0:T(8,128)}) custom-call(bf16[512,768]{1,0:T(8,128)(2,1)} %get-tuple-element.8.refs_0_, bf16[512,768]{1,0:T(8,128)(2,1)} %get-tuple-element.9.refs_1_, bf16[512,768]{1,0:T(8,128)(2,1)} %get-tuple-element.10.refs_2_, ...), custom_call_target="tpu_custom_call" | custom-call | tf_op jit(solution)/shard_map/place/pallas_call | solution.py:420
